TPU v7x, 32 devices: a whole 2x2x4 slice. The times are simulated.
32 devices in a mesh: layers: 2 (over y), tok: 4 (over z), feat: 4 (over x, core).
Axes of the slice: x: 2, y: 2, z: 4, core: 2. Of those that a mesh axis runs over, the one named last changes fastest.
Arguments:
- tokens: bfloat16 [4096, 16384], P(('layers', 'tok'), 'feat'), parts along dimension 0, may hold values from -24 to 24
- sketch: bfloat16 [512, 16384], P(None, 'feat'), may hold values from -0.001953125 to 0.001953125
- start: bfloat16 [32, 16384], P(None, 'feat'), may hold values from -8 to 8
Outputs:
- basis: float32 [192, 16384], P('layers', 'feat'), parts along dimension 0
- projected: float32 [192, 64], P('layers'), parts along dimension 0
There are 2 independent parts, one for each index of `layers`. A program takes and returns all parts, laid end to end along the dimension named above; an argument that names none is the same for every part. Nothing has to cross between parts.
All inputs are finite; a program needn't handle non-finite values.
Results may differ from a plain program's by a relative error of at most 0.008.
Values sent between devices are 32-bit elements; how exact they have to be, the bound alone decides.
A program may use at most 64 MiB of HBM per device.

v0:
```python
import jax
import jax.numpy as jnp
from jax import lax
from jax.sharding import PartitionSpec as P

B = 32
ITERS = 2


def orth_block(rows, sketched):
    gram = jnp.dot(sketched, sketched.T, precision=lax.Precision.HIGHEST)
    lower = jnp.linalg.cholesky(gram)
    new_rows = jax.scipy.linalg.solve_triangular(lower, rows, lower=True)
    new_sketched = jax.scipy.linalg.solve_triangular(lower, sketched, lower=True)
    return (new_rows, new_sketched, lower)


def project_coeffs(basis_sk, image_sk):
    return jnp.dot(basis_sk, image_sk.T, precision=lax.Precision.HIGHEST)


def apply_sketch(rows, sketch_part):
    return lax.dot_general(
        rows,
        sketch_part.astype(jnp.float32),
        (((1,), (1,)), ((), ())),
        precision=lax.Precision.HIGHEST,
        preferred_element_type=jnp.float32,
    )


def per_device(tokens, sketch, start):
    tok_rows, feat_width = tokens.shape
    total_tokens = tok_rows * lax.axis_size("tok")
    first = start.astype(jnp.float32)
    sketched = lax.psum(apply_sketch(first, sketch), "feat")
    block, block_sk, lower = orth_block(first, sketched)
    blocks = [block]
    sketches = [block_sk]
    columns = []
    total = (ITERS + 1) * B
    for step in range(ITERS):
        half = block.astype(jnp.bfloat16)
        rows_part = lax.dot_general(
            half, tokens, (((1,), (1,)), ((), ())), preferred_element_type=jnp.float32
        )
        rows_t = (lax.psum(rows_part, "feat") / total_tokens).astype(jnp.bfloat16)
        image_part = jnp.dot(rows_t, tokens, preferred_element_type=jnp.float32)
        basis = jnp.concatenate(blocks, 0)
        basis_sk = jnp.concatenate(sketches, 0)
        image = lax.psum(image_part, "tok")
        image_sk = lax.psum(apply_sketch(image, sketch), "feat")
        coeffs = project_coeffs(basis_sk, image_sk)
        resid = image - jnp.dot(coeffs.T, basis, precision=lax.Precision.HIGHEST)
        resid_sk = image_sk - jnp.dot(coeffs.T, basis_sk, precision=lax.Precision.HIGHEST)
        block, block_sk, lower = orth_block(resid, resid_sk)
        blocks.append(block)
        sketches.append(block_sk)
        filled = coeffs.shape[0]
        column = jnp.concatenate(
            [coeffs, lower.T, jnp.zeros((total - filled - B, B), jnp.float32)], 0
        )
        columns.append(column)
    return (jnp.concatenate(blocks, 0), jnp.concatenate(columns, 1))


def solution(mesh):
    placed = (P(("layers", "tok"), "feat"), P(None, "feat"), P(None, "feat"))
    return jax.shard_map(
        per_device,
        mesh=mesh,
        in_specs=placed,
        out_specs=(P("layers", "feat"), P("layers", None)),
        check_vma=False,
    )
```

profile of v0, /device:TPU:0, one launch (start us, length us, event | category | flops | bytes accessed | tf_op | source)
XLA Modules:
  0.0 314.9 jit_solution(14181747948842257809)
XLA Ops:
  7.2 4.3 %fusion.34 = f32[32,512]{1,0:T(8,128)} fusion(bf16[32,4096]{1,0:T(8,128)(2,1)} %param.10, bf16[512,4096]{1,0:T(8,128)(2,1)} %param.9), kind=kOutput, calls=%fused_computation.59 | convolution fusion | flops 134217728 | bytes 4521984 | tf_op jit(solution)/shard_map/dot_general | solution.py:23
  11.6 33.8 %all-reduce.8.cloned.1.call-done = f32[32,512]{1,0:T(8,128)} async-done(((f32[32,512]{1,0:T(8,128)}), f32[32,512]{1,0:T(8,128)}) %all-reduce.8.cloned.1.call-update) | async-done | bytes 65552 | tf_op jit(solution)/shard_map/psum | solution.py:36
  45.4 1.1 fusion.35
  46.6 2.9 cholesky.59
  50.9 2.4 custom-call.11
  54.0 4.2 %fusion.7 = f32[32,512]{1,0:T(8,128)} fusion(bf16[512,4096]{1,0:T(8,128)(2,1)} %param.8, f32[32,4096]{1,0:T(8,128)S(1)} %fusion.3), kind=kOutput, calls=%fused_computation.12 | convolution fusion | flops 134348800 | bytes 4784128 | tf_op jit(solution)/shard_map/dot_general | solution.py:44
  58.2 31.1 %all-reduce.10.cloned.1.call-done = f32[32,512]{1,0:T(8,128)} async-done(((f32[32,512]{1,0:T(8,128)}), f32[32,512]{1,0:T(8,128)}) %all-reduce.10.cloned.1.call-update) | async-done | bytes 65552 | tf_op jit(solution)/shard_map/psum | solution.py:47
  89.4 3.9 %fusion.10 = f32[32,4096]{1,0:T(8,128)} fusion(bf16[512,4096]{1,0:T(8,128)(2,1)} %param.8, f32[32,512]{1,0:T(8,128)} %all-reduce.10.cloned.1.call-done), kind=kOutput, calls=%fused_computation.18 | convolution fusion | flops 134250496 | bytes 4784128 | tf_op jit(solution)/shard_map/dot_general | solution.py:48
  93.3 38.4 %all-reduce.12.cloned.1.call-done = f32[32,4096]{1,0:T(8,128)} async-done(((f32[32,4096]{1,0:T(8,128)}), f32[32,4096]{1,0:T(8,128)}) %all-reduce.12.cloned.1.call-update) | async-done | bytes 524304 | tf_op jit(solution)/shard_map/psum | solution.py:51
  131.7 6.7 %fusion.36 = f32[32,512]{1,0:T(8,128)} fusion(f32[32,4096]{1,0:T(8,128)} %all-reduce.12.cloned.1.call-done, bf16[512,4096]{1,0:T(8,128)(2,1)} %param.9), kind=kOutput, calls=%fused_computation.61 | convolution fusion | flops 805306368 | bytes 4784128 | tf_op jit(solution)/shard_map/dot_general | solution.py:23
  138.8 30.9 %all-reduce.14.cloned.1.call-done = f32[32,512]{1,0:T(8,128)} async-done(((f32[32,512]{1,0:T(8,128)}), f32[32,512]{1,0:T(8,128)}) %all-reduce.14.cloned.1.call-update) | async-done | bytes 65552 | tf_op jit(solution)/shard_map/psum | solution.py:52
  170.7 1.0 convolution_subtract_fusion.3
  172.1 2.9 cholesky.70
  176.3 2.4 custom-call.13
  180.0 4.2 %fusion.5 = f32[32,512]{1,0:T(8,128)} fusion(bf16[512,4096]{1,0:T(8,128)(2,1)} %param.8, f32[32,4096]{1,0:T(8,128)S(1)} %fusion.20), kind=kOutput, calls=%fused_computation.10 | convolution fusion | flops 134348800 | bytes 4784128 | tf_op jit(solution)/shard_map/dot_general | solution.py:44
  184.2 31.2 %all-reduce.16.cloned.1.call-done = f32[32,512]{1,0:T(8,128)} async-done(((f32[32,512]{1,0:T(8,128)}), f32[32,512]{1,0:T(8,128)}) %all-reduce.16.cloned.1.call-update) | async-done | bytes 65552 | tf_op jit(solution)/shard_map/psum | solution.py:47
  215.4 3.8 %fusion.11 = f32[32,4096]{1,0:T(8,128)} fusion(bf16[512,4096]{1,0:T(8,128)(2,1)} %param.8, f32[32,512]{1,0:T(8,128)} %all-reduce.16.cloned.1.call-done), kind=kOutput, calls=%fused_computation.19 | convolution fusion | flops 134250496 | bytes 4784128 | tf_op jit(solution)/shard_map/dot_general | solution.py:48
  219.5 38.2 %all-reduce.18.cloned.1.call-done = f32[32,4096]{1,0:T(8,128)} async-done(((f32[32,4096]{1,0:T(8,128)}), f32[32,4096]{1,0:T(8,128)}) %all-reduce.18.cloned.1.call-update) | async-done | bytes 524304 | tf_op jit(solution)/shard_map/psum | solution.py:51
  257.7 6.7 %fusion.39 = f32[32,512]{1,0:T(8,128)} fusion(f32[32,4096]{1,0:T(8,128)} %all-reduce.18.cloned.1.call-done, bf16[512,4096]{1,0:T(8,128)(2,1)} %param.9), kind=kOutput, calls=%fused_computation.64 | convolution fusion | flops 805306368 | bytes 4784128 | tf_op jit(solution)/shard_map/dot_general | solution.py:23
  264.8 30.9 %all-reduce.20.cloned.1.call-done = f32[32,512]{1,0:T(8,128)} async-done(((f32[32,512]{1,0:T(8,128)}), f32[32,512]{1,0:T(8,128)}) %all-reduce.20.cloned.1.call-update) | async-done | bytes 65552 | tf_op jit(solution)/shard_map/psum | solution.py:52
  295.7 1.1 fusion.9
  298.1 2.9 cholesky.81
  302.4 2.4 custom-call.15
  306.1 1.3 pad_maximum_fusion
  (50 shorter events, 11.6 us)
Async XLA Ops:
  7.2 46.2 %copy-start.2 = (bf16[32,4096]{1,0:T(8,128)(2,1)S(1)}, bf16[32,4096]{1,0:T(8,128)(2,1)}, u32[]{:S(2)}) copy-start(bf16[32,4096]{1,0:T(8,128)(2,1)} %param.10) | copy-start | bytes 786436
  7.2 38.3 %all-reduce.8.cloned.1.call-start = ((), (), s32[]{:S(2)}) async-start(), calls=%async_computation | async-start | bytes 131072 | tf_op jit(solution)/shard_map/psum | solution.py:36
  11.5 77.8 %all-reduce.10.cloned.1.call-start = ((), (), s32[]{:S(2)}) async-start(), calls=%async_computation.1 | async-start | bytes 131072 | tf_op jit(solution)/shard_map/psum | solution.py:47
  58.2 80.4 %copy-start.3 = (f32[32,512]{1,0:T(8,128)S(1)}, f32[32,512]{1,0:T(8,128)}, u32[]{:S(2)}) copy-start(f32[32,512]{1,0:T(8,128)} %all-reduce.8.cloned.1.call-done) | copy-start | bytes 196612
  58.2 73.5 %all-reduce.12.cloned.1.call-start = ((), (), s32[]{:S(2)}) async-start(), calls=%async_computation.2 | async-start | bytes 1048576 | tf_op jit(solution)/shard_map/psum | solution.py:51
  93.3 76.4 %all-reduce.14.cloned.1.call-start = ((), (), s32[]{:S(2)}) async-start(), calls=%async_computation.3 | async-start | bytes 131072 | tf_op jit(solution)/shard_map/psum | solution.py:52
  131.7 47.0 %copy-start = (f32[32,4096]{1,0:T(8,128)S(1)}, f32[32,4096]{1,0:T(8,128)}, u32[]{:S(2)}) copy-start(f32[32,4096]{1,0:T(8,128)} %all-reduce.12.cloned.1.call-done) | copy-start | bytes 1572868
  138.5 76.9 %all-reduce.16.cloned.1.call-start = ((), (), s32[]{:S(2)}) async-start(), calls=%async_computation.4 | async-start | bytes 131072 | tf_op jit(solution)/shard_map/psum | solution.py:47
  184.2 73.5 %all-reduce.18.cloned.1.call-start = ((), (), s32[]{:S(2)}) async-start(), calls=%async_computation.5 | async-start | bytes 1048576 | tf_op jit(solution)/shard_map/psum | solution.py:51
  219.3 76.4 %all-reduce.20.cloned.1.call-start = ((), (), s32[]{:S(2)}) async-start(), calls=%async_computation.6 | async-start | bytes 131072 | tf_op jit(solution)/shard_map/psum | solution.py:52
  257.7 47.1 %copy-start.1 = (f32[32,4096]{1,0:T(8,128)S(1)}, f32[32,4096]{1,0:T(8,128)}, u32[]{:S(2)}) copy-start(f32[32,4096]{1,0:T(8,128)} %all-reduce.18.cloned.1.call-done) | copy-start | bytes 1572868
Sparse Core Ops, SparseCore 0:
  11.7 33.7 all-reduce.7
  58.3 31.0 all-reduce.9
  93.4 38.2 all-reduce.11
  138.6 31.0 all-reduce.13
  184.3 31.0 all-reduce.15
  219.4 38.2 all-reduce.17
  264.6 31.0 all-reduce.19
where the time goes:
time: 315 us
  waiting for transfers between devices  235 us (75%)
  matrix products  43.1 us (14%)
  other arithmetic  22 us (7%)
  between operations  14.3 us (5%)
    psum x2, waiting for transfers between devices, per_device(): image = lax.psum(image_part, 'tok')  76.6 us
    psum x2, waiting for transfers between devices, per_device(): rows_t = (lax.psum(rows_part, 'feat') / total_tokens).astype(jnp.bfloat16)  62.3 us
    psum x2, waiting for transfers between devices, per_device(): image_sk = lax.psum(apply_sketch(image, sketch), 'feat')  61.8 us
    psum x1, waiting for transfers between devices, per_device(): sketched = lax.psum(apply_sketch(first, sketch), 'feat')  33.8 us
    dot_general x3, matrix products, apply_sketch(): lax.dot_general(rows, sketch_part.astype(jnp.float32), (((1,), (1,)), (()...  17.8 us
    another operation x9, other arithmetic, orth_block(): lower = jnp.linalg.cholesky(gram)  10.8 us
    dot_general x2, matrix products, per_device(): lax.dot_general(half, tokens, (((1,), (1,)), ((), ())), preferred_element...  8.36 us
    another operation x4, other arithmetic, orth_block(): new_rows = jax.scipy.linalg.solve_triangular(lower, rows, lower=True)  7.96 us
  transfers between devices with their start and end apart: 7, of which 7 were waited for; matrix products, arithmetic and copies ran while one was open for 0% of the time, Pallas kernels for 0%

commit v1 on v0

v1 whole, which is shorter than its diff:
```python
import functools

import jax
import jax.numpy as jnp
from jax import lax
from jax.experimental import pallas as pl
from jax.experimental.pallas import tpu as pltpu
from jax.sharding import PartitionSpec as P

B = 32
ITERS = 2
LAG = 2
MESH = pl.DeviceIdType.MESH
EXACT = lax.Precision.HIGHEST
F32 = jnp.float32
BF16 = jnp.bfloat16


def dot_nn(a, b, precision=None):
    return jnp.dot(a, b, precision=precision, preferred_element_type=F32)


def dot_nt(a, b, precision=None):
    return lax.dot_general(
        a, b, (((1,), (1,)), ((), ())), precision=precision, preferred_element_type=F32
    )


def dot_tn(a, b, precision=None):
    return lax.dot_general(
        a, b, (((0,), (0,)), ((), ())), precision=precision, preferred_element_type=F32
    )


def halves(x):
    hi = x.astype(BF16)
    return hi, (x - hi.astype(F32)).astype(BF16)


def factor(gram):
    n = gram.shape[0]
    row = lax.broadcasted_iota(jnp.int32, (n, n), 0)
    col = lax.broadcasted_iota(jnp.int32, (n, n), 1)
    below = lax.broadcasted_iota(jnp.int32, (n, 1), 0)
    left, right = gram, jnp.where(row == col, 1.0, 0.0).astype(F32)
    for k in range(n - 1):
        inv = 1.0 / left[k : k + 1, k : k + 1]
        mult = jnp.where(below > k, left[:, k : k + 1], 0.0)
        left, right = (
            left - mult * (left[k : k + 1, :] * inv),
            right - mult * (right[k : k + 1, :] * inv),
        )
    diag = jnp.sum(jnp.where(row == col, left, 0.0), axis=1, keepdims=True)
    scale = 1.0 / jnp.sqrt(diag)
    return jnp.where(col >= row, left * scale, 0.0), right * scale


def kernel(
    tsize, fsize, tokens, sketch, start, basis, projected,
    tok, sk, st, sketched_tok, own, rbuf, sbuf, xbuf, stack, yv, zacc, kept, small,
    load_sem, chain_send, chain_recv, ex_send, ex_recv, out_sem,
):
    chunks, rows, width = tok.shape
    t, f = lax.axis_index("tok"), lax.axis_index("feat")
    scale = 1.0 / (rows * tsize)

    barrier = pltpu.get_barrier_semaphore()
    for d in range(1, fsize):
        pl.semaphore_signal(
            barrier, inc=1, device_id={"feat": lax.rem(f + d, fsize)}, device_id_type=MESH
        )

    @pl.when(t > 0)
    def _():
        pl.semaphore_signal(barrier, inc=1, device_id={"tok": t - 1}, device_id_type=MESH)

    @pl.when(t < tsize - 1)
    def _():
        pl.semaphore_signal(barrier, inc=1, device_id={"tok": t + 1}, device_id_type=MESH)

    def load(kind, c):
        cols = pl.ds(c * width, width)
        src, dst = ((start, st), (sketch, sk), (tokens, tok))[kind]
        return pltpu.make_async_copy(src.at[:, cols], dst.at[c], load_sem.at[kind, c])

    for c in range(chunks):
        load(0, c).start()
        load(1, c).start()
    for c in range(chunks):
        load(2, c).start()

    def exchange(phase, slot, peer):
        return pltpu.make_async_remote_copy(
            src_ref=xbuf.at[phase, slot],
            dst_ref=xbuf.at[phase, slot],
            send_sem=ex_send.at[phase, peer],
            recv_sem=ex_recv.at[phase, slot],
            device_id={"feat": peer},
            device_id_type=MESH,
        )

    def spread(phase, value):
        xbuf[phase, f] = value
        for d in range(1, fsize):
            exchange(phase, f, lax.rem(f + d, fsize)).start()

    def collect(phase):
        for d in range(1, fsize):
            peer = lax.rem(f + d, fsize)
            exchange(phase, peer, peer).wait_recv()
        total = xbuf[phase, 0]
        for k in range(1, fsize):
            total = total + xbuf[phase, k]
        return total

    part = jnp.zeros((B, width), F32)
    for c in range(chunks):
        load(0, c).wait()
        load(1, c).wait()
        part = part + dot_nt(st[c], sk[c])

    beside = jnp.where(t > 0, 1, 0) + jnp.where(t < tsize - 1, 1, 0)
    pl.semaphore_wait(barrier, fsize - 1 + beside)

    spread(0, part)
    part = jnp.zeros((B, rows), F32)
    for c in range(chunks):
        load(2, c).wait()
        part = part + dot_nt(st[c], tok[c])
    spread(1, part)

    def sketch_tokens(c, _):
        @pl.when(c == 0)
        def _():
            own_t[...] = dot_nt(tok[c], sk[c])

        @pl.when(c > 0)
        def _():
            own_t[...] += dot_nt(tok[c], sk[c])

        return 0

    own_t = sketched_tok
    lax.fori_loop(0, chunks, sketch_tokens, 0)

    def chain(step, way, slot):
        ahead = t + 1 if way == 0 else t - 1
        src = sbuf.at[step, way, slot]
        return pltpu.make_async_remote_copy(
            src_ref=src,
            dst_ref=rbuf.at[step, way, slot],
            send_sem=chain_send.at[step, way, slot],
            recv_sem=chain_recv.at[step, way, slot],
            device_id={"tok": ahead},
            device_id_type=MESH,
        )

    p_sum = collect(0)
    upper, linv = factor(dot_nt(p_sum, p_sum, EXACT))
    kept[0] = dot_nn(linv, p_sum, EXACT)
    small[0] = linv
    u_sum = collect(1)
    u_now = dot_nn(linv, u_sum, EXACT)
    zacc[1] = u_now
    yv[...] = (u_now * scale).astype(BF16)

    def pipeline(step):
        t_hi, t_lo = halves(sketched_tok[...])
        own[0] = dot_nn(yv[...], t_hi) + dot_nn(yv[...], t_lo)
        if step == 0:
            zacc[0] = jnp.zeros((B, rows), F32)
        lag_r = t * LAG
        lag_l = (tsize - 1 - t) * LAG
        lag_m = jnp.maximum(lag_r, lag_l)

        def body(i, _):
            @pl.when(jnp.logical_and(i >= 1, i <= chunks))
            def _():
                own[i] = dot_nn(yv[...], tok[i - 1])

            for way, lag, first, last in (
                (0, lag_r, t == 0, t == tsize - 1),
                (1, lag_l, t == tsize - 1, t == 0),
            ):
                slot = i - lag

                @pl.when(jnp.logical_and(slot >= 0, slot <= chunks))
                def _():
                    @pl.when(first)
                    def _():
                        sbuf[step, way, slot] = own[slot]
                        chain(step, way, slot).start()

                    @pl.when(jnp.logical_not(first))
                    def _():
                        chain(step, way, slot).wait_recv()

                        @pl.when(jnp.logical_not(last))
                        def _():
                            sbuf[step, way, slot] = own[slot] + rbuf[step, way, slot]
                            chain(step, way, slot).start()

            done = i - lag_m

            @pl.when(jnp.logical_and(done >= 0, done <= chunks))
            def _():
                @pl.when(t == 0)
                def _():
                    own[done] = own[done] + rbuf[step, 1, done]

                @pl.when(t == tsize - 1)
                def _():
                    own[done] = own[done] + rbuf[step, 0, done]

                @pl.when(jnp.logical_and(t > 0, t < tsize - 1))
                def _():
                    own[done] = own[done] + rbuf[step, 0, done] + rbuf[step, 1, done]

                @pl.when(done == 0)
                def _():
                    spread(2 + 2 * step, own[0])

                @pl.when(done > 0)
                def _():
                    c = done - 1
                    image = own[done]
                    if step == 0:
                        stack[c, 2 * B :, :] = image
                        hi, lo = halves(image)
                        zacc[0] += dot_nt(hi, tok[c]) + dot_nt(lo, tok[c])
                        stack[c, :B, :] = dot_nn(small[0], st[c].astype(F32), EXACT)
                    else:
                        block = dot_nn(small[1], stack[c, :B, :], EXACT) + dot_nn(
                            small[2], stack[c, 2 * B :, :], EXACT
                        )
                        stack[c, B : 2 * B, :] = block
                        stack[c, 2 * B :, :] = image

            return 0

        lax.fori_loop(0, chunks + 1 + LAG * (tsize - 1), body, 0)

    pipeline(0)
    spread(3, zacc[0])
    image_sk = collect(2)
    coeffs = dot_nt(kept[0], image_sk, EXACT)
    resid_sk = image_sk - dot_tn(coeffs, kept[0], EXACT)
    upper, linv = factor(dot_nt(resid_sk, resid_sk, EXACT))
    kept[1] = dot_nn(linv, resid_sk, EXACT)
    small[1] = -dot_nt(linv, coeffs, EXACT)
    small[2] = linv
    projected[:B, :B] = coeffs
    projected[B : 2 * B, :B] = upper
    projected[2 * B :, :B] = jnp.zeros((B, B), F32)
    z_sum = collect(3)
    yv[...] = (
        dot_nn(linv, z_sum - dot_tn(coeffs, zacc[1], EXACT), EXACT) * scale
    ).astype(BF16)

    pipeline(1)
    image_sk = collect(4)
    first_co = dot_nt(kept[0], image_sk, EXACT)
    second_co = dot_nt(kept[1], image_sk, EXACT)
    resid_sk = (
        image_sk - dot_tn(first_co, kept[0], EXACT) - dot_tn(second_co, kept[1], EXACT)
    )
    upper, linv = factor(dot_nt(resid_sk, resid_sk, EXACT))
    projected[:B, B:] = first_co
    projected[B : 2 * B, B:] = second_co
    projected[2 * B :, B:] = upper
    small[0] = -dot_nt(linv, first_co, EXACT)
    small[1] = -dot_nt(linv, second_co, EXACT)
    small[2] = linv

    def write(c):
        return pltpu.make_async_copy(
            stack.at[c],
            basis.at[:, pl.ds(pl.multiple_of(c * width, width), width)],
            out_sem.at[c],
        )

    for c in range(chunks):
        block = dot_nn(small[0], stack[c, :B, :], EXACT)
        block += dot_nn(small[1], stack[c, B : 2 * B, :], EXACT)
        block += dot_nn(small[2], stack[c, 2 * B :, :], EXACT)
        stack[c, 2 * B :, :] = block
        write(c).start()

    for phase in range(1 + 2 * ITERS):
        for d in range(1, fsize):
            exchange(phase, f, lax.rem(f + d, fsize)).wait_send()

    def drain(slot, _):
        for step in range(ITERS):

            @pl.when(t < tsize - 1)
            def _():
                chain(step, 0, slot).wait_send()

            @pl.when(t > 0)
            def _():
                chain(step, 1, slot).wait_send()

        return 0

    lax.fori_loop(0, chunks + 1, drain, 0)
    for c in range(chunks):
        write(c).wait()


def per_device(tsize, fsize, tokens, sketch, start):
    rows, features = tokens.shape
    width = sketch.shape[0]
    chunks = features // width
    total = (ITERS + 1) * B
    any_spec = pl.BlockSpec(memory_space=pl.ANY)
    return pl.pallas_call(
        functools.partial(kernel, tsize, fsize),
        out_shape=(
            jax.ShapeDtypeStruct((total, features), F32),
            jax.ShapeDtypeStruct((total, ITERS * B), F32),
        ),
        in_specs=[any_spec] * 3,
        out_specs=(any_spec, pl.BlockSpec(memory_space=pltpu.VMEM)),
        scratch_shapes=[
            pltpu.VMEM((chunks, rows, width), BF16),
            pltpu.VMEM((chunks, width, width), BF16),
            pltpu.VMEM((chunks, B, width), BF16),
            pltpu.VMEM((rows, width), F32),
            pltpu.VMEM((chunks + 1, B, width), F32),
            pltpu.VMEM((ITERS, 2, chunks + 1, B, width), F32),
            pltpu.VMEM((ITERS, 2, chunks + 1, B, width), F32),
            pltpu.VMEM((1 + 2 * ITERS, fsize, B, width), F32),
            pltpu.VMEM((chunks, total, width), F32),
            pltpu.VMEM((B, rows), BF16),
            pltpu.VMEM((2, B, rows), F32),
            pltpu.VMEM((2, B, width), F32),
            pltpu.VMEM((3, B, B), F32),
            pltpu.SemaphoreType.DMA((3, chunks)),
            pltpu.SemaphoreType.DMA((ITERS, 2, chunks + 1)),
            pltpu.SemaphoreType.DMA((ITERS, 2, chunks + 1)),
            pltpu.SemaphoreType.DMA((1 + 2 * ITERS, fsize)),
            pltpu.SemaphoreType.DMA((1 + 2 * ITERS, fsize)),
            pltpu.SemaphoreType.DMA((chunks,)),
        ],
        compiler_params=pltpu.CompilerParams(
            collective_id=0, has_side_effects=True, vmem_limit_bytes=48 * 1024 * 1024
        ),
    )(tokens, sketch, start)


def solution(mesh):
    placed = (P(("layers", "tok"), "feat"), P(None, "feat"), P(None, "feat"))
    return jax.shard_map(
        functools.partial(per_device, mesh.shape["tok"], mesh.shape["feat"]),
        mesh=mesh,
        in_specs=placed,
        out_specs=(P("layers", "feat"), P("layers", None)),
        check_vma=False,
    )
```

time: 315 us -> 79.9 us (0.25)
  waiting for transfers between devices: 235 us -> 0 us
  Pallas kernels: 0 us -> 74.1 us
  matrix products: 43.1 us -> 0 us
  other arithmetic: 22 us -> 0 us
  between operations: 14.3 us -> 0.65 us
  local copies, waits for them, and re-layouts: 0.23 us -> 4.97 us
    psum x7 -> x0, waiting for transfers between devices: 235 us -> none  [the longest x2 76.6 us: per_device(): image = lax.psum(image_part, 'tok')]
    pallas_call x0 -> x1, Pallas kernels: none -> 74.1 us  [per_device(): pl.pallas_call(functools.partial(kernel, tsize, fsize), out_shape=(jax.Sh...]
    dot_general x16 -> x0, matrix products: 40.7 us -> none  [the longest x3 17.8 us: apply_sketch(): lax.dot_general(rows, sketch_part.astype(jnp.float32), (((1,), (1,)), (()...]
    another operation x13 -> x0, other arithmetic: 18.7 us -> none  [the longest x9 10.8 us: orth_block(): lower = jnp.linalg.cholesky(gram)]
    unnamed x8 -> x5, local copies, waits for them, and re-layouts: 0.02 us -> 4.27 us
  transfers between devices with their start and end apart: 7 -> 0, of which waited for: 7 -> 0; matrix products, arithmetic and copies ran while one was open for 0% -> 0% of each run, Pallas kernels for 0% -> 0%
where the time goes in v1:
time: 79.9 us; the launch traced here: 79.7 us
  Pallas kernels  74.1 us (93%)
  local copies, waits for them, and re-layouts  4.97 us (6%)
    pallas_call x1, Pallas kernels, per_device(): pl.pallas_call(functools.partial(kernel, tsize, fsize), out_shape=(jax.Sh...  74.1 us
    unnamed x5, local copies, waits for them, and re-layouts  4.27 us

profile of v1, /device:TPU:0, one launch (start us, length us, event | category | flops | bytes accessed | tf_op | source)
XLA Modules:
  0.0 79.7 jit_solution(5916828157866581350)
XLA Ops:
  0.6 0.0 copy-start
  0.6 2.2 %copy-done = bf16[512,4096]{1,0:T(8,128)(2,1)S(1)} copy-done((bf16[512,4096]{1,0:T(8,128)(2,1)S(1)}, bf16[512,4096]{1,0:T(8,128)(2,1)}, u32[]{:S(2)}) %copy-start) | copy-done | bytes 4194328
  2.8 0.0 copy-start.1
  2.8 0.9 %copy-done.1 = bf16[32,4096]{1,0:T(8,128)(2,1)S(1)} copy-done((bf16[32,4096]{1,0:T(8,128)(2,1)S(1)}, bf16[32,4096]{1,0:T(8,128)(2,1)}, u32[]{:S(2)}) %copy-start.1) | copy-done | bytes 262168
  3.8 74.1 %shard_map.50 = (f32[96,4096]{1,0:T(8,128)S(1)}, f32[96,64]{1,0:T(8,128)S(1)}) custom-call(bf16[512,4096]{1,0:T(8,128)(2,1)S(1)} %copy-done, bf16[512,4096]{1,0:T(8,128)(2,1)} %sketch.1, bf16[32,4096]{1,0:T(8,128)(2,1)S(1)} %copy-done.1), custom_call_target="tpu_custom_call" | custom-call | tf_op jit(solution)/shard_map/pallas_call | solution.py:317
  77.9 0.7 copy.5
  78.6 1.1 %copy.7 = f32[96,4096]{1,0:T(8,128)} copy(f32[96,4096]{1,0:T(8,128)S(1)} %get-tuple-element.6) | data formatting | bytes 3145728
Async XLA Ops:
  0.6 2.2 %copy-start = (bf16[512,4096]{1,0:T(8,128)(2,1)S(1)}, bf16[512,4096]{1,0:T(8,128)(2,1)}, u32[]{:S(2)}) copy-start(bf16[512,4096]{1,0:T(8,128)(2,1)} %tokens.1) | copy-start | bytes 12582916
  2.8 0.9 %copy-start.1 = (bf16[32,4096]{1,0:T(8,128)(2,1)S(1)}, bf16[32,4096]{1,0:T(8,128)(2,1)}, u32[]{:S(2)}) copy-start(bf16[32,4096]{1,0:T(8,128)(2,1)} %start.1) | copy-start | bytes 786436

commit v2 on v1

--- a/solution.py
+++ b/solution.py
@@ -9,7 +9,9 @@
 
 B = 32
 ITERS = 2
-LAG = 2
+LAG = 3
+WAIT = 3
+STAGES = 5
 MESH = pl.DeviceIdType.MESH
 EXACT = lax.Precision.HIGHEST
 F32 = jnp.float32
@@ -37,19 +39,32 @@
     return hi, (x - hi.astype(F32)).astype(BF16)
 
 
-def factor(gram):
-    n = gram.shape[0]
-    row = lax.broadcasted_iota(jnp.int32, (n, n), 0)
-    col = lax.broadcasted_iota(jnp.int32, (n, n), 1)
-    below = lax.broadcasted_iota(jnp.int32, (n, 1), 0)
-    left, right = gram, jnp.where(row == col, 1.0, 0.0).astype(F32)
-    for k in range(n - 1):
+def grid_iota(n):
+    return (
+        lax.broadcasted_iota(jnp.int32, (n, n), 0),
+        lax.broadcasted_iota(jnp.int32, (n, n), 1),
+    )
+
+
+def eliminate(left, right, first, last):
+    below = lax.broadcasted_iota(jnp.int32, (left.shape[0], 1), 0)
+    for k in range(first, last):
         inv = 1.0 / left[k : k + 1, k : k + 1]
         mult = jnp.where(below > k, left[:, k : k + 1], 0.0)
         left, right = (
             left - mult * (left[k : k + 1, :] * inv),
             right - mult * (right[k : k + 1, :] * inv),
         )
+    return left, right
+
+
+def identity(n):
+    row, col = grid_iota(n)
+    return jnp.where(row == col, 1.0, 0.0).astype(F32)
+
+
+def finish(left, right):
+    row, col = grid_iota(left.shape[0])
     diag = jnp.sum(jnp.where(row == col, left, 0.0), axis=1, keepdims=True)
     scale = 1.0 / jnp.sqrt(diag)
     return jnp.where(col >= row, left * scale, 0.0), right * scale
@@ -57,7 +72,7 @@
 
 def kernel(
     tsize, fsize, tokens, sketch, start, basis, projected,
-    tok, sk, st, sketched_tok, own, rbuf, sbuf, xbuf, stack, yv, zacc, kept, small,
+    tok, sk, st, sketched_tok, own, rbuf, sbuf, xbuf, stack, yv, zacc, kept, small, work, cof,
     load_sem, chain_send, chain_recv, ex_send, ex_recv, out_sem,
 ):
     chunks, rows, width = tok.shape
@@ -156,13 +171,43 @@
         )
 
     p_sum = collect(0)
-    upper, linv = factor(dot_nt(p_sum, p_sum, EXACT))
+    upper, linv = finish(*eliminate(dot_nt(p_sum, p_sum, EXACT), identity(B), 0, B - 1))
     kept[0] = dot_nn(linv, p_sum, EXACT)
     small[0] = linv
     u_sum = collect(1)
     u_now = dot_nn(linv, u_sum, EXACT)
     zacc[1] = u_now
     yv[...] = (u_now * scale).astype(BF16)
+
+    def advance(step, stage):
+        if stage == 0:
+            image_sk = collect(2 + 2 * step)
+            kept[2] = image_sk
+            for j in range(step + 1):
+                cof[j] = dot_nt(kept[j], image_sk, EXACT)
+        elif stage == 1:
+            resid_sk = kept[2]
+            for j in range(step + 1):
+                resid_sk = resid_sk - dot_tn(cof[j], kept[j], EXACT)
+            kept[2] = resid_sk
+        elif stage == 2:
+            resid_sk = kept[2]
+            gram = dot_nt(resid_sk, resid_sk, EXACT)
+            work[0], work[1] = eliminate(gram, identity(B), 0, 8)
+        elif stage == 3:
+            work[0], work[1] = eliminate(work[0], work[1], 8, 20)
+        else:
+            upper, linv = finish(*eliminate(work[0], work[1], 20, B - 1))
+            place = slice(step * B, (step + 1) * B)
+            for j in range(step + 1):
+                projected[j * B : (j + 1) * B, place] = cof[j]
+                small[1 + 2 * step + j] = -dot_nt(linv, cof[j], EXACT)
+            projected[(step + 1) * B : (step + 2) * B, place] = upper
+            small[2 + 3 * step] = linv
+            if step == 0:
+                projected[2 * B :, place] = jnp.zeros((B, B), F32)
+                kept[1] = dot_nn(linv, kept[2], EXACT)
+                zacc[1] = dot_nn(small[1], zacc[1], EXACT)
 
     def pipeline(step):
         t_hi, t_lo = halves(sketched_tok[...])
@@ -236,41 +281,24 @@
                         stack[c, B : 2 * B, :] = block
                         stack[c, 2 * B :, :] = image
 
+            for stage in range(STAGES):
+
+                @pl.when(i == lag_m + WAIT + stage)
+                def _():
+                    advance(step, stage)
+
             return 0
 
-        lax.fori_loop(0, chunks + 1 + LAG * (tsize - 1), body, 0)
+        turns = max(chunks + 1, WAIT + STAGES) + LAG * (tsize - 1)
+        lax.fori_loop(0, turns, body, 0)
 
     pipeline(0)
     spread(3, zacc[0])
-    image_sk = collect(2)
-    coeffs = dot_nt(kept[0], image_sk, EXACT)
-    resid_sk = image_sk - dot_tn(coeffs, kept[0], EXACT)
-    upper, linv = factor(dot_nt(resid_sk, resid_sk, EXACT))
-    kept[1] = dot_nn(linv, resid_sk, EXACT)
-    small[1] = -dot_nt(linv, coeffs, EXACT)
-    small[2] = linv
-    projected[:B, :B] = coeffs
-    projected[B : 2 * B, :B] = upper
-    projected[2 * B :, :B] = jnp.zeros((B, B), F32)
     z_sum = collect(3)
-    yv[...] = (
-        dot_nn(linv, z_sum - dot_tn(coeffs, zacc[1], EXACT), EXACT) * scale
-    ).astype(BF16)
+    yv[...] = ((dot_nn(small[2], z_sum, EXACT) + zacc[1]) * scale).astype(BF16)
 
     pipeline(1)
-    image_sk = collect(4)
-    first_co = dot_nt(kept[0], image_sk, EXACT)
-    second_co = dot_nt(kept[1], image_sk, EXACT)
-    resid_sk = (
-        image_sk - dot_tn(first_co, kept[0], EXACT) - dot_tn(second_co, kept[1], EXACT)
-    )
-    upper, linv = factor(dot_nt(resid_sk, resid_sk, EXACT))
-    projected[:B, B:] = first_co
-    projected[B : 2 * B, B:] = second_co
-    projected[2 * B :, B:] = upper
-    small[0] = -dot_nt(linv, first_co, EXACT)
-    small[1] = -dot_nt(linv, second_co, EXACT)
-    small[2] = linv
+    last = jnp.concatenate([small[3], small[4], small[5]], 1)
 
     def write(c):
         return pltpu.make_async_copy(
@@ -280,9 +308,7 @@
         )
 
     for c in range(chunks):
-        block = dot_nn(small[0], stack[c, :B, :], EXACT)
-        block += dot_nn(small[1], stack[c, B : 2 * B, :], EXACT)
-        block += dot_nn(small[2], stack[c, 2 * B :, :], EXACT)
+        block = dot_nn(last, stack[c], EXACT)
         stack[c, 2 * B :, :] = block
         write(c).start()
 
@@ -334,8 +360,10 @@
             pltpu.VMEM((chunks, total, width), F32),
             pltpu.VMEM((B, rows), BF16),
             pltpu.VMEM((2, B, rows), F32),
-            pltpu.VMEM((2, B, width), F32),
-            pltpu.VMEM((3, B, B), F32),
+            pltpu.VMEM((3, B, width), F32),
+            pltpu.VMEM((6, B, B), F32),
+            pltpu.VMEM((2, B, B), F32),
+            pltpu.VMEM((ITERS, B, B), F32),
             pltpu.SemaphoreType.DMA((3, chunks)),
             pltpu.SemaphoreType.DMA((ITERS, 2, chunks + 1)),
             pltpu.SemaphoreType.DMA((ITERS, 2, chunks + 1)),
@@ -344,7 +372,7 @@
             pltpu.SemaphoreType.DMA((chunks,)),
         ],
         compiler_params=pltpu.CompilerParams(
-            collective_id=0, has_side_effects=True, vmem_limit_bytes=48 * 1024 * 1024
+            collective_id=0, has_side_effects=True, vmem_limit_bytes=60 * 1024 * 1024
         ),
     )(tokens, sketch, start)
 

time: 79.9 us -> 74 us (0.926)
  Pallas kernels: 74.1 us -> 69.1 us
  local copies, waits for them, and re-layouts: 4.97 us -> 4.15 us
    pallas_call x1, Pallas kernels: 74.1 us -> 69.1 us  [per_device(): pl.pallas_call(functools.partial(kernel, tsize, fsize), out_shape=(jax.Sh...]
    unnamed x5 -> x1, local copies, waits for them, and re-layouts: 4.27 us -> 2.65 us
where the time goes in v2:
time: 74 us; the launch traced here: 73.8 us
  Pallas kernels  69.1 us (93%)
  local copies, waits for them, and re-layouts  4.15 us (6%)
    pallas_call x1, Pallas kernels, per_device(): pl.pallas_call(functools.partial(kernel, tsize, fsize), out_shape=(jax.Sh...  69.1 us
    unnamed x1, local copies, waits for them, and re-layouts  2.65 us
    pallas_call x1, local copies, waits for them, and re-layouts, per_device(): pl.pallas_call(functools.partial(kernel, tsize, fsize), out_shape=(jax.Sh...  1.5 us

profile of v2, /device:TPU:0, one launch (start us, length us, event | category | flops | bytes accessed | tf_op | source)
XLA Modules:
  0.0 73.8 jit_solution(16409766084826939926)
XLA Ops:
  0.6 69.1 %shard_map.50 = (f32[96,4096]{1,0:T(8,128)}, f32[96,64]{1,0:T(8,128)}) custom-call(bf16[512,4096]{1,0:T(8,128)(2,1)} %tokens.1, bf16[512,4096]{1,0:T(8,128)(2,1)} %sketch.1, bf16[32,4096]{1,0:T(8,128)(2,1)} %start.1), custom_call_target="tpu_custom_call" | custom-call | tf_op jit(solution)/shard_map/pallas_call | solution.py:343
  69.7 1.5 %copy.5 = f32[96,64]{0,1:T(8,128)} copy(f32[96,64]{1,0:T(8,128)} %get-tuple-element.3) | data formatting | bytes 49152 | tf_op jit(solution)/shard_map/pallas_call | solution.py:343
  71.2 2.7 %copy.7 = f32[96,4096]{1,0:T(8,128)} copy(f32[96,4096]{1,0:T(8,128)} %get-tuple-element.6) | data formatting | bytes 3145728

commit v3 on v2

--- a/solution.py
+++ b/solution.py
@@ -25,12 +25,6 @@
 def dot_nt(a, b, precision=None):
     return lax.dot_general(
         a, b, (((1,), (1,)), ((), ())), precision=precision, preferred_element_type=F32
-    )
-
-
-def dot_tn(a, b, precision=None):
-    return lax.dot_general(
-        a, b, (((0,), (0,)), ((), ())), precision=precision, preferred_element_type=F32
     )
 
 
@@ -184,11 +178,11 @@
             image_sk = collect(2 + 2 * step)
             kept[2] = image_sk
             for j in range(step + 1):
-                cof[j] = dot_nt(kept[j], image_sk, EXACT)
+                cof[j] = dot_nt(image_sk, kept[j], EXACT)
         elif stage == 1:
             resid_sk = kept[2]
             for j in range(step + 1):
-                resid_sk = resid_sk - dot_tn(cof[j], kept[j], EXACT)
+                resid_sk = resid_sk - dot_nn(cof[j], kept[j], EXACT)
             kept[2] = resid_sk
         elif stage == 2:
             resid_sk = kept[2]
@@ -200,12 +194,12 @@
             upper, linv = finish(*eliminate(work[0], work[1], 20, B - 1))
             place = slice(step * B, (step + 1) * B)
             for j in range(step + 1):
-                projected[j * B : (j + 1) * B, place] = cof[j]
-                small[1 + 2 * step + j] = -dot_nt(linv, cof[j], EXACT)
-            projected[(step + 1) * B : (step + 2) * B, place] = upper
+                projected[place, j * B : (j + 1) * B] = cof[j]
+                small[1 + 2 * step + j] = -dot_nn(linv, cof[j], EXACT)
+            projected[place, (step + 1) * B : (step + 2) * B] = dot_nt(identity(B), upper, EXACT)
             small[2 + 3 * step] = linv
             if step == 0:
-                projected[2 * B :, place] = jnp.zeros((B, B), F32)
+                projected[place, 2 * B :] = jnp.zeros((B, B), F32)
                 kept[1] = dot_nn(linv, kept[2], EXACT)
                 zacc[1] = dot_nn(small[1], zacc[1], EXACT)
 
@@ -340,11 +334,11 @@
     chunks = features // width
     total = (ITERS + 1) * B
     any_spec = pl.BlockSpec(memory_space=pl.ANY)
-    return pl.pallas_call(
+    basis, projected = pl.pallas_call(
         functools.partial(kernel, tsize, fsize),
         out_shape=(
             jax.ShapeDtypeStruct((total, features), F32),
-            jax.ShapeDtypeStruct((total, ITERS * B), F32),
+            jax.ShapeDtypeStruct((ITERS * B, total), F32),
         ),
         in_specs=[any_spec] * 3,
         out_specs=(any_spec, pl.BlockSpec(memory_space=pltpu.VMEM)),
@@ -375,6 +369,7 @@
             collective_id=0, has_side_effects=True, vmem_limit_bytes=60 * 1024 * 1024
         ),
     )(tokens, sketch, start)
+    return basis, projected.T
 
 
 def solution(mesh):

time: 74 us -> 74.1 us (level)
    pallas_call x1 -> x0, local copies, waits for them, and re-layouts: 1.5 us -> none  [per_device(): pl.pallas_call(functools.partial(kernel, tsize, fsize), out_shape=(jax.Sh...]
    unnamed x1 -> x2, local copies, waits for them, and re-layouts: 2.65 us -> 4.03 us
where the time goes in v3:
time: 74.1 us; the launch traced here: 73.9 us
  Pallas kernels  69.2 us (93%)
  local copies, waits for them, and re-layouts  4.03 us (5%)
    pallas_call x1, Pallas kernels, per_device(): pl.pallas_call(functools.partial(kernel, tsize, fsize), out_shape=(jax.Sh...  69.2 us
    unnamed x2, local copies, waits for them, and re-layouts  4.03 us

profile of v3, /device:TPU:0, one launch (start us, length us, event | category | flops | bytes accessed | tf_op | source)
XLA Modules:
  0.0 73.9 jit_solution(3539096681071235707)
XLA Ops:
  0.6 69.2 %shard_map.50 = (f32[96,4096]{1,0:T(8,128)}, f32[64,96]{1,0:T(8,128)}) custom-call(bf16[512,4096]{1,0:T(8,128)(2,1)} %tokens.1, bf16[512,4096]{1,0:T(8,128)(2,1)} %sketch.1, bf16[32,4096]{1,0:T(8,128)(2,1)} %start.1), custom_call_target="tpu_custom_call" | custom-call | tf_op jit(solution)/shard_map/pallas_call | solution.py:337
  69.8 2.7 %copy.7 = f32[96,4096]{1,0:T(8,128)} copy(f32[96,4096]{1,0:T(8,128)} %get-tuple-element.8) | data formatting | bytes 3145728
  72.5 1.4 %copy.8 = f32[96,64]{0,1:T(8,128)} copy(f32[96,64]{0,1:T(8,128)} %bitcast.1) | data formatting | bytes 49152
